TPU v7x, 128 devices: a whole 4x4x4 slice. The times are simulated.
128 devices in a mesh: group: 8 (over y, core), index: 16 (over z, x).
Axes of the slice: x: 4, y: 4, z: 4, core: 2. Of those that a mesh axis runs over, the one named last changes fastest.
Arguments:
- acts: bfloat16 [8192, 4096], P(('group', 'index')), may hold values from -6 to 6
- enc_weight: bfloat16 [4096, 16384], P(None, 'index'), may hold values from -0.09375 to 0.09375
- enc_bias: float32 [16384], P('index'), may hold values from -3 to 3
- dec_weight: bfloat16 [16384, 4096], P('index'), may hold values from -0.1875 to 0.1875
- dec_bias: float32 [4096], replicated, may hold values from -3 to 3
- active: int32 [128, 32], P('group'), may hold values from 0 to 255, all different within a row
- counts: int32 [128], P('group'), may hold values from 1 to 32
Outputs:
- reconstruction: bfloat16 [8192, 4096], P(('group', 'index'))
- dec_grad: float32 [16384, 4096], P(('index', 'group'))
Inputs may be any that keep to these rules, and one draw needn't show every extreme that they name: `active`: only the first counts[r] entries of row r are live; the entries of a row are distinct.
All inputs are finite; a program needn't handle non-finite values.
Results may differ from a plain program's by a relative error of at most 0.015.
Values may be sent and summed in bfloat16 or wider, within the bound.
No kernel may reach another device: no remote copies, remote signals or barrier semaphores. Data moves between devices by JAX's collectives and lax.ppermute only.
A program may use at most 128 MiB of HBM per device.

v0:
```python
import jax
import jax.numpy as jnp
from jax import lax
from jax.sharding import PartitionSpec as P

BLOCK = 64


def body(acts, enc_weight, enc_bias, dec_weight, dec_bias, active, counts):
    tok_dev = acts.shape[0]
    lat_dev = dec_weight.shape[0]
    my_index = lax.axis_index("index")
    own_count = lat_dev // BLOCK
    own_blocks = my_index * own_count + jnp.arange(own_count)
    slots = jnp.arange(active.shape[1])[None, :] < counts[:, None]
    matches = (active[:, :, None] == own_blocks[None, None, :]) & slots[:, :, None]
    block_live = jnp.any(matches, axis=1).astype(jnp.float32)
    latent_live = jnp.repeat(block_live, BLOCK, axis=1)
    row_live = jnp.repeat(latent_live, tok_dev, axis=0)
    rows = lax.all_gather(acts, "index", axis=0, tiled=True)
    preact = jnp.dot(rows, enc_weight, preferred_element_type=jnp.float32) + enc_bias
    codes = jnp.where(row_live > 0.0, jnp.maximum(preact, 0.0), 0.0).astype(jnp.bfloat16)
    summed = lax.psum_scatter(
        jnp.dot(codes, dec_weight, preferred_element_type=jnp.float32).astype(jnp.bfloat16),
        "index",
        scatter_dimension=0,
        tiled=True,
    ).astype(jnp.float32)
    recon_mine = (summed + dec_bias).astype(jnp.bfloat16)
    error_mine = (recon_mine.astype(jnp.float32) - acts.astype(jnp.float32)).astype(jnp.bfloat16)
    error_all = lax.all_gather(error_mine, "index", axis=0, tiled=True)
    grad_local = lax.dot_general(
        codes, error_all, (((0,), (0,)), ((), ())), preferred_element_type=jnp.float32
    )
    dec_grad = lax.psum_scatter(
        grad_local.astype(jnp.bfloat16), "group", scatter_dimension=0, tiled=True
    ).astype(jnp.float32)
    return (recon_mine, dec_grad)


def solution(mesh):
    in_specs = (
        P(("group", "index"), None),
        P(None, "index"),
        P("index"),
        P("index", None),
        P(),
        P("group", None),
        P("group"),
    )
    out_specs = (P(("group", "index"), None), P(("index", "group"), None))
    return jax.shard_map(body, mesh=mesh, in_specs=in_specs, out_specs=out_specs, check_vma=False)
```

profile of v0, /device:TPU:9, one launch (start us, length us, event | category | flops | bytes accessed | tf_op | source)
XLA Modules:
  0.0 344.2 jit_solution(13828106759440546288)
XLA Ops:
  7.2 0.0 all-gather.3.cloned.1.call-start
  7.2 0.7 all-gather.3.cloned.1.call-update
  7.9 0.0 reduce-scatter.3.cloned.1.call-start
  8.0 0.7 iota_compare_fusion
  8.7 1.1 and_reduce_fusion
  9.8 0.1 broadcast_in_dim.5
  9.9 0.1 gt.12
  10.1 73.3 %all-gather.3.cloned.1.call-done = bf16[1024,4096]{1,0:T(8,128)(2,1)} async-done(((bf16[64,4096]{1,0:T(8,128)(2,1)}), bf16[1024,4096]{1,0:T(8,128)(2,1)}) %all-gather.3.cloned.1.call-update) | async-done | bytes 8388624 | tf_op jit(solution)/shard_map/all_gather | solution.py:20
  83.3 13.7 %select_convert_fusion = bf16[1024,1024]{1,0:T(8,128)(2,1)S(1)} fusion(f32[1024]{0:T(1024)} %param.9, pred[16,1024]{1,0:T(8,128)(4,1)S(1)} %gt.12, bf16[1024,4096]{1,0:T(8,128)(2,1)} %all-gather.3.cloned.1.call-done, bf16[4096,1024]{1,0:T(8,128)(2,1)} %param.8), kind=kOutput, calls=%fused_computation.2 | convolution fusion | flops 8594128896 | bytes 18894848 | tf_op jit(solution)/shard_map/dot_general | solution.py:21
  97.0 14.2 %convolution_convert_fusion.1 = bf16[1024,4096]{1,0:T(8,128)(2,1)} fusion(bf16[1024,1024]{1,0:T(8,128)(2,1)S(1)} %select_convert_fusion, bf16[1024,4096]{1,0:T(8,128)(2,1)} %param.10), kind=kOutput, calls=%fused_computation.1 | convolution fusion | flops 8594128896 | bytes 18874368 | tf_op jit(solution)/shard_map/dot_general | solution.py:24
  111.3 0.0 copy-start
  111.3 0.0 copy-start.1
  111.3 0.0 reduce-scatter.3.cloned.1.call-update
  111.3 0.0 all-gather.5.cloned.1.call-start
  111.3 83.6 %reduce-scatter.3.cloned.1.call-done = bf16[64,4096]{1,0:T(8,128)(2,1)} async-done(((bf16[1024,4096]{1,0:T(8,128)(2,1)}), bf16[64,4096]{1,0:T(8,128)(2,1)}) %reduce-scatter.3.cloned.1.call-update) | async-done | bytes 524304 | tf_op jit(solution)/shard_map/reduce_scatter | solution.py:23
  194.9 0.0 copy-done
  195.0 0.0 copy-done.1
  195.0 2.2 subtract_convert_fusion
  197.2 0.0 all-gather.5.cloned.1.call-update
  197.2 0.0 reduce-scatter.5.cloned.1.call-start
  197.2 71.8 %all-gather.5.cloned.1.call-done = bf16[1024,4096]{1,0:T(8,128)(2,1)} async-done(((bf16[64,4096]{1,0:T(8,128)(2,1)}), bf16[1024,4096]{1,0:T(8,128)(2,1)}) %all-gather.5.cloned.1.call-update) | async-done | bytes 8388624 | tf_op jit(solution)/shard_map/all_gather | solution.py:31
  269.0 14.5 %convolution_convert_fusion = bf16[1024,4096]{1,0:T(8,128)(2,1)} fusion(bf16[1024,1024]{1,0:T(8,128)(2,1)S(1)} %select_convert_fusion, bf16[1024,4096]{1,0:T(8,128)(2,1)} %all-gather.5.cloned.1.call-done), kind=kOutput, calls=%fused_computation | convolution fusion | flops 8594128896 | bytes 18874368 | tf_op jit(solution)/shard_map/dot_general | solution.py:32
  283.5 0.0 reduce-scatter.5.cloned.1.call-update
  283.6 51.3 %reduce-scatter.5.cloned.1.call-done = bf16[128,4096]{1,0:T(8,128)(2,1)} async-done(((bf16[1024,4096]{1,0:T(8,128)(2,1)}), bf16[128,4096]{1,0:T(8,128)(2,1)}) %reduce-scatter.5.cloned.1.call-update) | async-done | bytes 1048592 | tf_op jit(solution)/shard_map/reduce_scatter | solution.py:35
  334.9 2.8 convert_element_type.39
  (2 shorter events, 0.0 us)
Async XLA Ops:
  7.2 76.2 %all-gather.3.cloned.1.call-start = ((), (), s32[]{:S(2)}) async-start(), calls=%async_computation.2 | async-start | bytes 8912896 | tf_op jit(solution)/shard_map/all_gather | solution.py:20
  7.9 187.1 %reduce-scatter.3.cloned.1.call-start = ((), (), s32[]{:S(2)}) async-start(), calls=%async_computation.3 | async-start | bytes 8912896 | tf_op jit(solution)/shard_map/reduce_scatter | solution.py:23
  111.3 83.7 %copy-start = (bf16[64,4096]{1,0:T(8,128)(2,1)S(1)}, bf16[64,4096]{1,0:T(8,128)(2,1)}, u32[]{:S(2)}) copy-start(bf16[64,4096]{1,0:T(8,128)(2,1)} %param.7) | copy-start | bytes 1572868
  111.3 83.7 %copy-start.1 = (f32[4096]{0:T(1024)S(1)}, f32[4096]{0:T(1024)}, u32[]{:S(2)}) copy-start(f32[4096]{0:T(1024)} %param.11) | copy-start | bytes 49156
  111.3 157.7 %all-gather.5.cloned.1.call-start = ((), (), s32[]{:S(2)}) async-start(), calls=%async_computation.4 | async-start | bytes 8912896 | tf_op jit(solution)/shard_map/all_gather | solution.py:31
  197.2 137.7 %reduce-scatter.5.cloned.1.call-start = ((), (), s32[]{:S(2)}) async-start(), calls=%async_computation.5 | async-start | bytes 9437184 | tf_op jit(solution)/shard_map/reduce_scatter | solution.py:35
Sparse Core Ops, SparseCore 0:
  10.1 73.1 all-gather.2
  111.4 83.4 reduce-scatter.2
  197.7 71.2 all-gather.4
  283.7 51.1 reduce-scatter.4
where the time goes:
time: 346 us; the launch traced here: 344 us
  waiting for transfers between devices  281 us (81%)
  matrix products  42.5 us (12%)
  between operations  13.8 us (4%)
  other arithmetic  6.81 us (2%)
    reduce_scatter x1, waiting for transfers between devices, body(): lax.psum_scatter(jnp.dot(codes, dec_weight, preferred_element_type=jnp.fl...  83.6 us
    all_gather x1, waiting for transfers between devices, body(): rows = lax.all_gather(acts, 'index', axis=0, tiled=True)  73.3 us
    all_gather x1, waiting for transfers between devices, body(): error_all = lax.all_gather(error_mine, 'index', axis=0, tiled=True)  71.8 us
    reduce_scatter x1, waiting for transfers between devices, body(): lax.psum_scatter(grad_local.astype(jnp.bfloat16), 'group', scatter_dimens...  51.3 us
    dot_general x1, matrix products, body(): lax.dot_general(codes, error_all, (((0,), (0,)), ((), ())), preferred_ele...  14.5 us
    dot_general x1, matrix products, body(): jnp.dot(codes, dec_weight, preferred_element_type=jnp.float32)  14.2 us
    dot_general x1, matrix products, body(): jnp.dot(rows, enc_weight, preferred_element_type=jnp.float32) + enc_bias  13.7 us
  transfers between devices with their start and end apart: 4, of which 4 were waited for; matrix products, arithmetic and copies ran while one was open for 1% of the time, Pallas kernels for 0%

commit v1 on v0

v1 whole, which is shorter than its diff:
```python
import jax
import jax.numpy as jnp
from jax import lax
from jax.experimental import pallas as pl
from jax.experimental.pallas import tpu as pltpu
from jax.sharding import PartitionSpec as P

BLOCK = 64
SIDE = 4
CAP = 48
AXES = ("group", "index")
F32 = jnp.float32
BF16 = jnp.bfloat16
I32 = jnp.int32


def device_of(y, core, z, x):
    return ((y * 2 + core) * SIDE + z) * SIDE + x


def ring_pairs(axis):
    pairs = []
    for y in range(SIDE):
        for core in range(2):
            for z in range(SIDE):
                for x in range(SIDE):
                    at = {"y": y, "z": z, "x": x}
                    to = dict(at)
                    to[axis] = (at[axis] + (1 if core == 0 else -1)) % SIDE
                    pairs.append(
                        (device_of(y, core, z, x), device_of(to["y"], core, to["z"], to["x"]))
                    )
    return pairs


RINGS = {axis: ring_pairs(axis) for axis in ("x", "y", "z")}


def hop(block, axis):
    return lax.ppermute(block, AXES, RINGS[axis])


def ring_gather(block, axis):
    blocks = {0: block}
    for o in (3, 2, 1):
        block = hop(block, axis)
        blocks[o] = block
    return jnp.concatenate([blocks[o] for o in range(SIDE)], axis=0)


def pack_kernel(pair_ref, codes_ref, out_ref):
    left = lax.broadcasted_iota(I32, (BLOCK // 2, 2 * BLOCK), 1) < BLOCK

    def one(j, carry):
        pair = pair_ref[j]
        row = pl.multiple_of((pair // 16) * BLOCK, BLOCK)
        col = pl.multiple_of(((pair % 16) // 2) * (2 * BLOCK), 2 * BLOCK)
        tile = codes_ref[pl.ds(row, BLOCK), pl.ds(col, 2 * BLOCK)].astype(F32)
        turned = pltpu.roll(tile, BLOCK, 1)
        odd = pair % 2 == 1
        to_left = jnp.where(odd, turned, tile)
        to_right = jnp.where(odd, tile, turned)
        packed = jnp.where(left, to_left[: BLOCK // 2], to_right[BLOCK // 2 :])
        out_ref[pl.ds(pl.multiple_of(j * (BLOCK // 2), BLOCK // 2), BLOCK // 2), :] = packed.astype(BF16)
        return carry

    lax.fori_loop(0, CAP, one, 0)


def pack(pairs, codes):
    return pl.pallas_call(
        pack_kernel,
        out_shape=jax.ShapeDtypeStruct((CAP * BLOCK // 2, 2 * BLOCK), BF16),
        in_specs=[
            pl.BlockSpec(memory_space=pltpu.SMEM),
            pl.BlockSpec(memory_space=pltpu.VMEM),
        ],
        out_specs=pl.BlockSpec(memory_space=pltpu.VMEM),
        compiler_params=pltpu.CompilerParams(vmem_limit_bytes=16 * 2**20),
    )(pairs, codes)


def place(block):
    return pl.multiple_of((((block % 16) // 2) * 16 + block // 16) * (2 * BLOCK) + (block % 2) * BLOCK, BLOCK)


def slice_kernel(active_ref, slot_ref, counts_ref, packed_ref, dec_ref, acts_ref, bias_ref, recon_ref, grad_ref, lhs_ref, total_ref):
    half = BLOCK // 2
    cols = dec_ref.shape[1]
    rows = dec_ref.shape[0]
    left = lax.broadcasted_iota(I32, (half, 2 * BLOCK), 1) < BLOCK
    step = 512

    def clear(j, carry):
        total_ref[pl.ds(pl.multiple_of(j * step, step), step), :] = jnp.zeros((step, cols), F32)
        return carry

    lax.fori_loop(0, rows // step, clear, 0)

    def row_block(r, carry):
        count = counts_ref[r]
        quads = (count + 3) // 4

        def load(s):
            slot = slot_ref[r, s]
            tile = packed_ref[pl.ds(pl.multiple_of(slot * half, half), half), :].astype(F32)
            return jnp.where(s < count, tile, 0.0)

        def pair(s):
            first, second = load(s), load(s + 1)
            top = jnp.where(left, first, pltpu.roll(second, BLOCK, 1))
            bottom = jnp.where(left, pltpu.roll(first, BLOCK, 1), second)
            return jnp.concatenate([top, bottom], axis=0)

        def decode(q, total):
            s = q * 4
            lhs = jnp.concatenate([pair(s), pair(s + 2)], axis=1).astype(BF16)
            lhs_ref[q] = lhs
            dec = jnp.concatenate([dec_ref[pl.ds(place(active_ref[r, s + k]), BLOCK), :] for k in range(4)], axis=0)
            return total + jnp.dot(lhs, dec, preferred_element_type=F32)

        at = pl.ds(pl.multiple_of(r * BLOCK, BLOCK), BLOCK)
        total = lax.fori_loop(0, quads, decode, jnp.zeros((BLOCK, cols), F32))
        recon = (total + bias_ref[...]).astype(BF16)
        recon_ref[at, :] = recon
        error = (recon.astype(F32) - acts_ref[at, :].astype(F32)).astype(BF16)

        def gradient(q, carry):
            s = q * 4
            part = lax.dot_general(lhs_ref[q], error, (((0,), (0,)), ((), ())), preferred_element_type=F32)
            for k in range(4):
                to = pl.ds(place(active_ref[r, s + k]), BLOCK)
                total_ref[to, :] += part[k * BLOCK : (k + 1) * BLOCK]
            return carry

        lax.fori_loop(0, quads, gradient, 0)
        return carry

    lax.fori_loop(0, counts_ref.shape[0], row_block, 0)

    def narrow(j, carry):
        at = pl.ds(pl.multiple_of(j * step, step), step)
        grad_ref[at, :] = total_ref[at, :].astype(BF16)
        return carry

    lax.fori_loop(0, rows // step, narrow, 0)


def column_slice(active, slot, counts, packed, dec, acts, bias):
    rows, cols = dec.shape
    tokens = acts.shape[0]
    slots = active.shape[1]
    smem = pl.BlockSpec(memory_space=pltpu.SMEM)
    vmem = pl.BlockSpec(memory_space=pltpu.VMEM)
    return pl.pallas_call(
        slice_kernel,
        out_shape=(
            jax.ShapeDtypeStruct((tokens, cols), BF16),
            jax.ShapeDtypeStruct((rows, cols), BF16),
        ),
        in_specs=[smem, smem, smem, vmem, vmem, vmem, vmem],
        out_specs=(vmem, vmem),
        scratch_shapes=[
            pltpu.VMEM((slots // 4, BLOCK, 4 * BLOCK), BF16),
            pltpu.VMEM((rows, cols), F32),
        ],
        compiler_params=pltpu.CompilerParams(vmem_limit_bytes=56 * 2**20),
    )(active, slot, counts, packed, dec, acts, bias)


def body(acts, enc_weight, enc_bias, dec_weight, dec_bias, active, counts):
    tok_dev, width = acts.shape
    lat_dev = dec_weight.shape[0]
    n_index = lax.axis_size("index")
    n_group = lax.axis_size("group")
    cols = width // n_index
    part = lat_dev // n_group
    own_count = lat_dev // BLOCK
    n_blocks = own_count * n_index
    my_index = lax.axis_index("index")
    my_group = lax.axis_index("group")
    my_z, my_x = my_index // SIDE, my_index % SIDE
    ahead = jnp.where(my_group % 2 == 0, 1, SIDE - 1)

    rows = lax.all_gather(acts, "index", axis=0, tiled=True)

    mine = lax.dynamic_slice_in_dim(dec_weight, my_group * part, part, axis=0)
    mine = mine.reshape(part, n_index, cols).transpose(1, 0, 2)
    mine = lax.all_to_all(mine, "index", 0, 0, tiled=True)
    dec_cols = lax.all_gather(mine.reshape(n_index * part, cols), "group", axis=0, tiled=True)

    slots = jnp.arange(active.shape[1])[None, :] < counts[:, None]
    is_block = active[:, :, None] == jnp.arange(n_blocks)[None, None, :]
    live = jnp.any(is_block & slots[:, :, None], axis=1)
    by_owner = live.reshape(n_index, n_index, own_count).transpose(1, 0, 2).reshape(n_index, n_index * own_count)
    pair_at = jnp.arange(n_index * own_count)
    upto = (pair_at[:, None] <= pair_at[None, :]).astype(BF16)
    ranks = jnp.dot(by_owner.astype(BF16), upto, preferred_element_type=F32).astype(I32)
    most = jnp.max(ranks[:, -1])
    most = lax.pmax(most, "group")
    ranks = jnp.where(by_owner, ranks - 1, -1)

    own_ranks = lax.dynamic_index_in_dim(ranks, my_index, 0, keepdims=False)
    pairs = jnp.sum(
        jnp.where(own_ranks[None, :] == jnp.arange(CAP)[:, None], pair_at[None, :], 0), axis=1
    ).astype(I32)

    owner = jnp.arange(n_index)
    dz = (ahead * (owner // SIDE - my_z + SIDE)) % SIDE
    dx = (ahead * (owner % SIDE - my_x + SIDE)) % SIDE
    half = CAP // 2
    first = ((dz * SIDE + dx) * half)[:, None] + ranks
    second = ((n_index + dx * SIDE + dz) * half)[:, None] + ranks - half
    table = jnp.where(ranks < half, first, second)
    table = table.reshape(n_index, n_index, own_count).transpose(1, 0, 2).reshape(n_index, n_blocks)
    slot = jnp.sum(jnp.where(is_block & slots[:, :, None], table[:, None, :], 0), axis=2).astype(I32)
    slot = jnp.clip(slot, 0, n_index * CAP - 1)

    preact = jnp.dot(rows, enc_weight, preferred_element_type=F32) + enc_bias
    codes_any = jnp.maximum(preact, 0.0).astype(BF16)

    def packed_path():
        packed = pack(pairs, codes_any)
        n = packed.shape[0] // 2
        one = ring_gather(ring_gather(packed[:n], "x"), "z")
        two = ring_gather(ring_gather(packed[n:], "z"), "x")
        packed = jnp.concatenate([one, two], axis=0)
        acts_cols = lax.dynamic_slice_in_dim(rows, my_index * cols, cols, axis=1)
        bias_cols = lax.dynamic_slice_in_dim(dec_bias, my_index * cols, cols, axis=0)[None, :]
        recon, grad = column_slice(active, slot, counts, packed, dec_cols, acts_cols, bias_cols)
        grad = lax.psum_scatter(grad, "group", scatter_dimension=0, tiled=True)
        recon = lax.all_to_all(recon.reshape(n_index, tok_dev, cols), "index", 0, 0, tiled=True)
        grad = lax.all_to_all(grad.reshape(n_index, part, cols), "index", 0, 0, tiled=True)
        recon = recon.transpose(1, 0, 2).reshape(tok_dev, width)
        grad = grad.transpose(1, 0, 2).reshape(part, width).astype(F32)
        return recon, grad

    def dense_path():
        own_live = lax.dynamic_slice_in_dim(live, my_index * own_count, own_count, axis=1)
        row_live = jnp.repeat(jnp.repeat(own_live, BLOCK, axis=1), tok_dev, axis=0)
        codes = jnp.where(row_live, codes_any, jnp.zeros((), BF16))
        summed = lax.psum_scatter(
            jnp.dot(codes, dec_weight, preferred_element_type=F32).astype(BF16),
            "index",
            scatter_dimension=0,
            tiled=True,
        ).astype(F32)
        recon = (summed + dec_bias).astype(BF16)
        error = (recon.astype(F32) - acts.astype(F32)).astype(BF16)
        error_all = lax.all_gather(error, "index", axis=0, tiled=True)
        grad = lax.dot_general(codes, error_all, (((0,), (0,)), ((), ())), preferred_element_type=F32)
        grad = lax.psum_scatter(grad.astype(BF16), "group", scatter_dimension=0, tiled=True)
        return recon, grad.astype(F32)

    return lax.cond(most <= CAP, packed_path, dense_path)


def solution(mesh):
    in_specs = (
        P(("group", "index"), None),
        P(None, "index"),
        P("index"),
        P("index", None),
        P(),
        P("group", None),
        P("group"),
    )
    out_specs = (P(("group", "index"), None), P(("index", "group"), None))
    return jax.shard_map(body, mesh=mesh, in_specs=in_specs, out_specs=out_specs, check_vma=False)
```

time: 346 us -> 359 us (1.038)
  waiting for transfers between devices: 281 us -> 157 us
  blocking collectives: 0 us -> 54.2 us
  Pallas kernels: 0 us -> 49.6 us
  starting transfers between devices: 0.16 us -> 42.7 us
  matrix products: 42.5 us -> 13.8 us
  local copies, waits for them, and re-layouts: 0.23 us -> 22.8 us
    reduce_scatter x2 -> x1, waiting for transfers between devices: 135 us -> 39.9 us  [packed_path(): grad = lax.psum_scatter(grad, 'group', scatter_dimension=0, tiled=True)]
    pallas_call x0 -> x2, Pallas kernels: none -> 49.6 us  [the longest x1 45.3 us: column_slice(): pl.pallas_call(slice_kernel, out_shape=(jax.ShapeDtypeStruct((tokens, col...]
    all_to_all x0 -> x2, blocking collectives: none -> 43.2 us  [the longest x1 27.5 us: body(): mine = lax.all_to_all(mine, 'index', 0, 0, tiled=True)]
    all_gather x1, waiting for transfers between devices: 73.3 us -> 35.7 us  [body(): rows = lax.all_gather(acts, 'index', axis=0, tiled=True)]
    ppermute x0 -> x12, starting transfers between devices: none -> 35.9 us  [hop(): return lax.ppermute(block, AXES, RINGS[axis])]
    all_gather x1, waiting for transfers between devices: 71.8 us -> 37.5 us  [body(): lax.all_gather(mine.reshape(n_index * part, cols), 'group', axis=0, tiled...]
    dot_general x3 -> x2, matrix products: 42.5 us -> 13.8 us  [the longest x1 13.7 us: body(): preact = jnp.dot(rows, enc_weight, preferred_element_type=F32) + enc_bias]
    ppermute x0 -> x12, waiting for transfers between devices: none -> 23.8 us  [hop(): return lax.ppermute(block, AXES, RINGS[axis])]
  transfers between devices with their start and end apart: 4 -> 16, of which waited for: 4 -> 11; matrix products, arithmetic and copies ran while one was open for 1% -> 9% of each run, Pallas kernels for 0% -> 0%
where the time goes in v1:
time: 359 us; the launch traced here: 358 us
  waiting for transfers between devices  157 us (44%)
  blocking collectives  54.2 us (15%)
  Pallas kernels  49.6 us (14%)
  starting transfers between devices  42.7 us (12%)
  local copies, waits for them, and re-layouts  22.8 us (6%)
  between operations  14.6 us (4%)
  matrix products  13.8 us (4%)
    pallas_call x1, Pallas kernels, column_slice(): pl.pallas_call(slice_kernel, out_shape=(jax.ShapeDtypeStruct((tokens, col...  45.3 us
    reduce_scatter x1, waiting for transfers between devices, packed_path(): grad = lax.psum_scatter(grad, 'group', scatter_dimension=0, tiled=True)  39.9 us
    all_gather x1, waiting for transfers between devices, body(): lax.all_gather(mine.reshape(n_index * part, cols), 'group', axis=0, tiled...  37.5 us
    ppermute x12, starting transfers between devices, hop(): return lax.ppermute(block, AXES, RINGS[axis])  35.9 us
    all_gather x1, waiting for transfers between devices, body(): rows = lax.all_gather(acts, 'index', axis=0, tiled=True)  35.7 us
    all_to_all x1, blocking collectives, body(): mine = lax.all_to_all(mine, 'index', 0, 0, tiled=True)  27.5 us
    ppermute x12, waiting for transfers between devices, hop(): return lax.ppermute(block, AXES, RINGS[axis])  23.8 us
    all_to_all x1, waiting for transfers between devices, packed_path(): lax.all_to_all(grad.reshape(n_index, part, cols), 'index', 0, 0, tiled=True)  19.2 us
  transfers between devices with their start and end apart: 16, of which 11 were waited for; matrix products, arithmetic and copies ran while one was open for 9% of the time, Pallas kernels for 0%

profile of v1, /device:TPU:9, one launch (start us, length us, event | category | flops | bytes accessed | tf_op | source)
XLA Modules:
  0.0 358.1 jit_solution(13514881348016396245)
XLA Ops:
  10.0 27.5 %all_to_all.14 = bf16[16,128,256]{1,2,0:T(8,128)(2,1)S(1)} all-to-all(bf16[16,128,256]{1,2,0:T(8,128)(2,1)S(1)} %bitcast.31), channel_id=1, replica_groups=mesh['group'=8,'index'=16] {'index'}, dimensions={0} | all-to-all | bytes 2097152 | tf_op jit(solution)/shard_map/all_to_all | solution.py:189
  40.3 11.0 %pmax.7 = s32[]{:T(128)} all-reduce(s32[]{:T(128)} %slice_reduce_fusion), channel_id=1, replica_groups=mesh['group'=8,'index'=16] {'group'}, use_global_device_ids=true, to_apply=%region_2.3 | all-reduce | flops 1 | bytes 8 | tf_op jit(solution)/shard_map/pmax | solution.py:200
  52.2 35.7 %all-gather.6.cloned.1.call-done = bf16[1024,4096]{1,0:T(8,128)(2,1)} async-done(((bf16[64,4096]{1,0:T(8,128)(2,1)}), bf16[1024,4096]{1,0:T(8,128)(2,1)}) %all-gather.6.cloned.1.call-update) | async-done | bytes 8388624 | tf_op jit(solution)/shard_map/all_gather | solution.py:185
  87.9 13.7 %maximum_convert_fusion = bf16[1024,1024]{1,0:T(8,128)(2,1)S(1)} fusion(f32[1024]{0:T(1024)S(1)} %copy-done.8, bf16[1024,4096]{1,0:T(8,128)(2,1)} %all-gather.6.cloned.1.call-done, bf16[4096,1024]{1,0:T(8,128)(2,1)} %param.10), kind=kOutput, calls=%fused_computation.28 | convolution fusion | flops 8593080320 | bytes 18878464 | tf_op jit(solution)/shard_map/dot_general | solution.py:219
  101.5 37.5 %all-gather.8.cloned.1.call-done = bf16[16384,256]{1,0:T(8,128)(2,1)} async-done(((bf16[2048,256]{1,0:T(8,128)(2,1)}), bf16[16384,256]{1,0:T(8,128)(2,1)}) %all-gather.8.cloned.1.call-update) | async-done | bytes 8388624 | tf_op jit(solution)/shard_map/all_gather | solution.py:190
  139.1 212.5 %conditional.3 = (bf16[64,4096]{1,0:T(8,128)(2,1)}, f32[128,4096]{1,0:T(8,128)}) conditional(s32[]{:T(128)} %convert_element_type.41, (s32[]{:T(128)}, pred[16,256]{1,0:T(8,128)(4,1)S(1)}, bf16[1024,1024]{1,0:T(8,128)(2,1)S(1)}, bf16[1024,4096]{1,0:T(8,128)(2,1)}, f32[4096]{0:T(1024)S(1)}, /*index=5*/bf16[64,4096]{1,0:T(8,128)(2,1)S(1)}) %tuple.62, ...), branch_computations={%region_3.6_spmd, %region_6.10_spmd} | conditional | flops 17191665664 | bytes 145835008
  139.5 4.3 %branch_1_fun.2 = bf16[1536,128]{1,0:T(8,128)(2,1)S(1)} custom-call(s32[48]{0:T(128)S(1)} %select_reduce_fusion.1.pair_ref, bf16[1024,1024]{1,0:T(8,128)(2,1)S(1)} %get-tuple-element.87.codes_ref), custom_call_target="tpu_custom_call" | custom-call | tf_op jit(solution)/shard_map/cond/branch_1_fun/pallas_call | solution.py:71
  144.6 2.4 collective-permute-start
  147.0 2.6 collective-permute-done
  149.6 3.1 collective-permute-start.1
  152.7 2.6 collective-permute-done.1
  155.3 3.1 collective-permute-start.2
  158.4 2.7 collective-permute-start.6
  161.2 2.7 collective-permute-start.3
  163.9 3.3 collective-permute-start.7
  167.1 7.8 %collective-permute-done.7 = bf16[768,128]{1,0:T(8,128)(2,1)S(1)} collective-permute-done((bf16[768,128]{1,0:T(8,128)(2,1)S(1)}, bf16[768,128]{1,0:T(8,128)(2,1)S(1)}, u32[]{:S(2)}, u32[]{:S(2)}) %collective-permute-start.7) | collective-permute-done | bytes 196640 | tf_op jit(solution)/shard_map/cond/branch_1_fun/ppermute | solution.py:40
  174.9 3.1 collective-permute-start.8
  178.0 2.6 collective-permute-done.8
  181.6 3.1 collective-permute-start.9
  184.7 3.1 collective-permute-start.4
  189.2 4.7 %collective-permute-done.9 = bf16[3072,128]{1,0:T(8,128)(2,1)S(1)} collective-permute-done((bf16[3072,128]{1,0:T(8,128)(2,1)}, bf16[3072,128]{1,0:T(8,128)(2,1)S(1)}, u32[]{:S(2)}, u32[]{:S(2)}) %collective-permute-start.9) | collective-permute-done | bytes 786464 | tf_op jit(solution)/shard_map/cond/branch_1_fun/ppermute | solution.py:40
  193.9 3.4 collective-permute-start.10
  197.3 2.8 collective-permute-start.5
  200.1 1.9 constant_dynamic-slice_fusion.2.acts_ref
  206.3 3.1 collective-permute-start.11
  210.3 2.1 constant_dynamic-update-slice_fusion.8
  216.1 2.2 collective-permute-done.11
  221.2 45.3 %branch_1_fun.3 = (bf16[1024,256]{1,0:T(8,128)(2,1)}, bf16[16384,256]{1,0:T(8,128)(2,1)}) custom-call(s32[16,32]{1,0:T(8,128)S(1)} %get-tuple-element.78.active_ref, s32[16,32]{1,0:T(8,128)} %broadcast_clamp_fusion.slot_ref, s32[16]{0:T(128)S(1)} %get-tuple-element.81.counts_ref, bf16[24576,128]{1,0:T(8,128)(2,1)} %constant_dynamic-update-slice_fusion.packed_ref, ...), custom_call_target="tpu_custom_call" | custom-call | tf_op jit(solution)/shard_map/cond/branch_1_fun/pallas_call | solution.py:155
  267.5 15.7 %all_to_all.13 = bf16[16,64,256]{2,1,0:T(8,128)(2,1)S(1)} all-to-all(bf16[16,64,256]{2,1,0:T(8,128)(2,1)S(1)} %bitcast.35), channel_id=1, replica_groups=mesh['group'=8,'index'=16] {'index'}, dimensions={0} | all-to-all | bytes 1048576 | tf_op jit(solution)/shard_map/cond/branch_1_fun/all_to_all | solution.py:232
  283.2 39.9 %reduce-scatter.8.cloned.1.call-done = bf16[2048,256]{1,0:T(8,128)(2,1)} async-done(((bf16[16384,256]{1,0:T(8,128)(2,1)}), bf16[2048,256]{1,0:T(8,128)(2,1)}) %reduce-scatter.8.cloned.1.call-update) | async-done | bytes 1048592 | tf_op jit(solution)/shard_map/cond/branch_1_fun/reduce_scatter | solution.py:231
  323.1 6.7 %all-to-all-start.1 = ((bf16[16,128,256]{2,1,0:T(8,128)(2,1)}), bf16[16,128,256]{2,1,0:T(8,128)(2,1)S(1)}, u32[]{:S(2)}, u32[]{:S(2)}) async-start(bf16[16,128,256]{2,1,0:T(8,128)(2,1)} %bitcast.34), calls=%async_computation.2 | async-start | bytes 2097152 | tf_op jit(solution)/shard_map/cond/branch_1_fun/all_to_all | solution.py:233
  330.6 19.2 %all-to-all-done.1 = bf16[16,128,256]{2,1,0:T(8,128)(2,1)S(1)} async-done(((bf16[16,128,256]{2,1,0:T(8,128)(2,1)}), bf16[16,128,256]{2,1,0:T(8,128)(2,1)S(1)}, u32[]{:S(2)}, u32[]{:S(2)}) %all-to-all-start.1) | async-done | bytes 1048608 | tf_op jit(solution)/shard_map/cond/branch_1_fun/all_to_all | solution.py:233
  (65 shorter events, 24.4 us)
Async XLA Ops:
  7.2 31.6 %copy-start.7 = (s32[16]{0:T(128)S(1)}, s32[16]{0:T(128)}, u32[]{:S(2)}) copy-start(s32[16]{0:T(128)} %param.15) | copy-start | bytes 196
  7.2 31.7 %copy-start.4 = (s32[16,32]{1,0:T(8,128)S(1)}, s32[16,32]{1,0:T(8,128)}, u32[]{:S(2)}) copy-start(s32[16,32]{1,0:T(8,128)} %param.14) | copy-start | bytes 6148
  7.2 80.7 %copy-start.8 = (f32[1024]{0:T(1024)S(1)}, f32[1024]{0:T(1024)}, u32[]{:S(2)}) copy-start(f32[1024]{0:T(1024)} %param.11) | copy-start | bytes 12292
  7.2 80.7 %all-gather.6.cloned.1.call-start = ((), (), s32[]{:S(2)}) async-start(), calls=%async_computation.10 | async-start | bytes 8912896 | tf_op jit(solution)/shard_map/all_gather | solution.py:185
  7.9 131.2 %all-gather.8.cloned.1.call-start = ((), (), s32[]{:S(2)}) async-start(), calls=%async_computation.11 | async-start | bytes 9437184 | tf_op jit(solution)/shard_map/all_gather | solution.py:190
  52.1 87.0 %copy-start.2 = (bf16[64,4096]{1,0:T(8,128)(2,1)S(1)}, bf16[64,4096]{1,0:T(8,128)(2,1)}, u32[]{:S(2)}) copy-start(bf16[64,4096]{1,0:T(8,128)(2,1)} %param.9) | copy-start | bytes 1572868
  52.2 87.0 %copy-start.5 = (f32[4096]{0:T(1024)S(1)}, f32[4096]{0:T(1024)}, u32[]{:S(2)}) copy-start(f32[4096]{0:T(1024)} %param.13) | copy-start | bytes 49156
  139.4 21.8 %copy-start.6 = (f32[4096]{0:T(1024)}, f32[4096]{0:T(1024)S(1)}, u32[]{:S(2)}) copy-start(f32[4096]{0:T(1024)S(1)} %get-tuple-element.90) | copy-start | bytes 49156 | tf_op jit(solution)/shard_map/conditional.1
  139.4 183.8 %reduce-scatter.8.cloned.1.call-start = ((), (), s32[]{:S(2)}) async-start(), calls=%async_computation.9 | async-start | bytes 9437184 | tf_op jit(solution)/shard_map/cond/branch_1_fun/reduce_scatter | solution.py:231
  144.6 5.0 %collective-permute-start = (bf16[768,128]{1,0:T(8,128)(2,1)S(1)}, bf16[768,128]{1,0:T(8,128)(2,1)S(1)}, u32[]{:S(2)}, u32[]{:S(2)}) collective-permute-start(bf16[768,128]{1,0:T(8,128)(2,1)S(1)} %get-tuple-element.106), channel_id=1, source_target_pairs={{0,1},{1,2},{2,3},{3,0},{4,5},{5,6},{6,7},{7,4},{8,9},{9,10},{10,1... | collective-permute-start | bytes 589832 | tf_op jit(solution)/shard_map/cond/branch_1_fun/ppermute | solution.py:40
  149.6 5.7 %collective-permute-start.1 = (bf16[768,128]{1,0:T(8,128)(2,1)S(1)}, bf16[768,128]{1,0:T(8,128)(2,1)S(1)}, u32[]{:S(2)}, u32[]{:S(2)}) collective-permute-start(bf16[768,128]{1,0:T(8,128)(2,1)S(1)} %collective-permute-done), channel_id=1, source_target_pairs={{0,1},{1,2},{2,3},{3,0},{4,5},{5,6},{6,7},{7,4},{8,9},{9,10},{10,1... | collective-permute-start | bytes 589832 | tf_op jit(solution)/shard_map/cond/branch_1_fun/ppermute | solution.py:40
  155.3 5.8 %collective-permute-start.2 = (bf16[768,128]{1,0:T(8,128)(2,1)S(1)}, bf16[768,128]{1,0:T(8,128)(2,1)S(1)}, u32[]{:S(2)}, u32[]{:S(2)}) collective-permute-start(bf16[768,128]{1,0:T(8,128)(2,1)S(1)} %collective-permute-done.1), channel_id=1, source_target_pairs={{0,1},{1,2},{2,3},{3,0},{4,5},{5,6},{6,7},{7,4},{8,9},{9,10},{10,1... | collective-permute-start | bytes 589832 | tf_op jit(solution)/shard_map/cond/branch_1_fun/ppermute | solution.py:40
  158.4 5.4 %collective-permute-start.6 = (bf16[768,128]{1,0:T(8,128)(2,1)S(1)}, bf16[768,128]{1,0:T(8,128)(2,1)S(1)}, u32[]{:S(2)}, u32[]{:S(2)}) collective-permute-start(bf16[768,128]{1,0:T(8,128)(2,1)S(1)} %get-tuple-element.104), channel_id=1, source_target_pairs={{0,4},{1,5},{2,6},{3,7},{4,8},{5,9},{6,10},{7,11},{8,12},{9,13},{1... | collective-permute-start | bytes 589832 | tf_op jit(solution)/shard_map/cond/branch_1_fun/ppermute | solution.py:40
  161.2 23.5 %collective-permute-start.3 = (bf16[3072,128]{1,0:T(8,128)(2,1)S(1)}, bf16[3072,128]{1,0:T(8,128)(2,1)S(1)}, u32[]{:S(2)}, u32[]{:S(2)}) collective-permute-start(bf16[3072,128]{1,0:T(8,128)(2,1)S(1)} %pad_maximum_fusion), channel_id=1, source_target_pairs={{0,4},{1,5},{2,6},{3,7},{4,8},{5,9},{6,10},{7,11},{8,12},{9,13},{1... | collective-permute-start | bytes 2359304 | tf_op jit(solution)/shard_map/cond/branch_1_fun/ppermute | solution.py:40
  163.9 11.0 %collective-permute-start.7 = (bf16[768,128]{1,0:T(8,128)(2,1)S(1)}, bf16[768,128]{1,0:T(8,128)(2,1)S(1)}, u32[]{:S(2)}, u32[]{:S(2)}) collective-permute-start(bf16[768,128]{1,0:T(8,128)(2,1)S(1)} %collective-permute-done.6), channel_id=1, source_target_pairs={{0,4},{1,5},{2,6},{3,7},{4,8},{5,9},{6,10},{7,11},{8,12},{9,13},{1... | collective-permute-start | bytes 589832 | tf_op jit(solution)/shard_map/cond/branch_1_fun/ppermute | solution.py:40
  174.9 5.7 %collective-permute-start.8 = (bf16[768,128]{1,0:T(8,128)(2,1)S(1)}, bf16[768,128]{1,0:T(8,128)(2,1)S(1)}, u32[]{:S(2)}, u32[]{:S(2)}) collective-permute-start(bf16[768,128]{1,0:T(8,128)(2,1)S(1)} %collective-permute-done.7), channel_id=1, source_target_pairs={{0,4},{1,5},{2,6},{3,7},{4,8},{5,9},{6,10},{7,11},{8,12},{9,13},{1... | collective-permute-start | bytes 589832 | tf_op jit(solution)/shard_map/cond/branch_1_fun/ppermute | solution.py:40
  181.6 12.4 %collective-permute-start.9 = (bf16[3072,128]{1,0:T(8,128)(2,1)}, bf16[3072,128]{1,0:T(8,128)(2,1)S(1)}, u32[]{:S(2)}, u32[]{:S(2)}) collective-permute-start(bf16[3072,128]{1,0:T(8,128)(2,1)} %pad_maximum_fusion.1), channel_id=1, source_target_pairs={{0,1},{1,2},{2,3},{3,0},{4,5},{5,6},{6,7},{7,4},{8,9},{9,10},{10,1... | collective-permute-start | bytes 2359304 | tf_op jit(solution)/shard_map/cond/branch_1_fun/ppermute | solution.py:40
  184.7 12.7 %collective-permute-start.4 = (bf16[3072,128]{1,0:T(8,128)(2,1)S(1)}, bf16[3072,128]{1,0:T(8,128)(2,1)}, u32[]{:S(2)}, u32[]{:S(2)}) collective-permute-start(bf16[3072,128]{1,0:T(8,128)(2,1)S(1)} %collective-permute-done.3), channel_id=1, source_target_pairs={{0,4},{1,5},{2,6},{3,7},{4,8},{5,9},{6,10},{7,11},{8,12},{9,13},{1... | collective-permute-start | bytes 2359304 | tf_op jit(solution)/shard_map/cond/branch_1_fun/ppermute | solution.py:40
  193.9 12.3 %collective-permute-start.10 = (bf16[3072,128]{1,0:T(8,128)(2,1)S(1)}, bf16[3072,128]{1,0:T(8,128)(2,1)S(1)}, u32[]{:S(2)}, u32[]{:S(2)}) collective-permute-start(bf16[3072,128]{1,0:T(8,128)(2,1)S(1)} %collective-permute-done.9), channel_id=1, source_target_pairs={{0,1},{1,2},{2,3},{3,0},{4,5},{5,6},{6,7},{7,4},{8,9},{9,10},{10,1... | collective-permute-start | bytes 2359304 | tf_op jit(solution)/shard_map/cond/branch_1_fun/ppermute | solution.py:40
  197.3 12.1 %collective-permute-start.5 = (bf16[3072,128]{1,0:T(8,128)(2,1)}, bf16[3072,128]{1,0:T(8,128)(2,1)S(1)}, u32[]{:S(2)}, u32[]{:S(2)}) collective-permute-start(bf16[3072,128]{1,0:T(8,128)(2,1)} %collective-permute-done.4), channel_id=1, source_target_pairs={{0,4},{1,5},{2,6},{3,7},{4,8},{5,9},{6,10},{7,11},{8,12},{9,13},{1... | collective-permute-start | bytes 2359304 | tf_op jit(solution)/shard_map/cond/branch_1_fun/ppermute | solution.py:40
  206.3 12.1 %collective-permute-start.11 = (bf16[3072,128]{1,0:T(8,128)(2,1)S(1)}, bf16[3072,128]{1,0:T(8,128)(2,1)S(1)}, u32[]{:S(2)}, u32[]{:S(2)}) collective-permute-start(bf16[3072,128]{1,0:T(8,128)(2,1)S(1)} %collective-permute-done.10), channel_id=1, source_target_pairs={{0,1},{1,2},{2,3},{3,0},{4,5},{5,6},{6,7},{7,4},{8,9},{9,10},{10,1... | collective-permute-start | bytes 2359304 | tf_op jit(solution)/shard_map/cond/branch_1_fun/ppermute | solution.py:40
  266.5 1.0 copy-start.3
  323.1 26.7 %all-to-all-start.1 = ((bf16[16,128,256]{2,1,0:T(8,128)(2,1)}), bf16[16,128,256]{2,1,0:T(8,128)(2,1)S(1)}, u32[]{:S(2)}, u32[]{:S(2)}) async-start(bf16[16,128,256]{2,1,0:T(8,128)(2,1)} %bitcast.34), calls=%async_computation.2 | async-start | bytes 2097152 | tf_op jit(solution)/shard_map/cond/branch_1_fun/all_to_all | solution.py:233
Sparse Core Ops, SparseCore 0:
  10.2 77.6 all-gather.5
  90.2 48.8 all-gather.7
  266.6 56.4 reduce-scatter.7

commit v2 on v1

--- a/solution.py
+++ b/solution.py
@@ -8,6 +8,7 @@
 BLOCK = 64
 SIDE = 4
 CAP = 48
+EIGHT = 8
 AXES = ("group", "index")
 F32 = jnp.float32
 BF16 = jnp.bfloat16
@@ -40,12 +41,13 @@
     return lax.ppermute(block, AXES, RINGS[axis])
 
 
-def ring_gather(block, axis):
-    blocks = {0: block}
+def ring_gather(blocks, axes):
+    slots = [{0: block} for block in blocks]
     for o in (3, 2, 1):
-        block = hop(block, axis)
-        blocks[o] = block
-    return jnp.concatenate([blocks[o] for o in range(SIDE)], axis=0)
+        blocks = lax.optimization_barrier([hop(block, axis) for block, axis in zip(blocks, axes)])
+        for slot, block in zip(slots, blocks):
+            slot[o] = block
+    return [[slot[o] for o in range(SIDE)] for slot in slots]
 
 
 def pack_kernel(pair_ref, codes_ref, out_ref):
@@ -84,22 +86,32 @@
     return pl.multiple_of((((block % 16) // 2) * 16 + block // 16) * (2 * BLOCK) + (block % 2) * BLOCK, BLOCK)
 
 
-def slice_kernel(active_ref, slot_ref, counts_ref, packed_ref, dec_ref, acts_ref, bias_ref, recon_ref, grad_ref, lhs_ref, total_ref):
+def slice_kernel(active_ref, slot_ref, counts_ref, acts_ref, bias_ref, dec_hbm, *refs):
+    pieces = refs[: 2 * SIDE]
+    recon_ref, grad_ref, packed_ref, dec_ref, lhs_ref, total_ref, sems = refs[2 * SIDE :]
     half = BLOCK // 2
-    cols = dec_ref.shape[1]
-    rows = dec_ref.shape[0]
+    rows, cols = dec_ref.shape
+    size = pieces[0].shape[0]
     left = lax.broadcasted_iota(I32, (half, 2 * BLOCK), 1) < BLOCK
     step = 512
 
+    copies = [pltpu.make_async_copy(dec_hbm, dec_ref, sems.at[2 * SIDE])]
+    for k, piece in enumerate(pieces):
+        copies.append(pltpu.make_async_copy(piece, packed_ref.at[pl.ds(k * size, size), :], sems.at[k]))
+    for copy in copies:
+        copy.start()
+
     def clear(j, carry):
         total_ref[pl.ds(pl.multiple_of(j * step, step), step), :] = jnp.zeros((step, cols), F32)
         return carry
 
     lax.fori_loop(0, rows // step, clear, 0)
+    for copy in copies:
+        copy.wait()
 
     def row_block(r, carry):
         count = counts_ref[r]
-        quads = (count + 3) // 4
+        steps = (count + EIGHT - 1) // EIGHT
 
         def load(s):
             slot = slot_ref[r, s]
@@ -113,27 +125,29 @@
             return jnp.concatenate([top, bottom], axis=0)
 
         def decode(q, total):
-            s = q * 4
-            lhs = jnp.concatenate([pair(s), pair(s + 2)], axis=1).astype(BF16)
+            s = q * EIGHT
+            lhs = jnp.concatenate([pair(s + k) for k in range(0, EIGHT, 2)], axis=1).astype(BF16)
             lhs_ref[q] = lhs
-            dec = jnp.concatenate([dec_ref[pl.ds(place(active_ref[r, s + k]), BLOCK), :] for k in range(4)], axis=0)
+            dec = jnp.concatenate(
+                [dec_ref[pl.ds(place(active_ref[r, s + k]), BLOCK), :] for k in range(EIGHT)], axis=0
+            )
             return total + jnp.dot(lhs, dec, preferred_element_type=F32)
 
         at = pl.ds(pl.multiple_of(r * BLOCK, BLOCK), BLOCK)
-        total = lax.fori_loop(0, quads, decode, jnp.zeros((BLOCK, cols), F32))
+        total = lax.fori_loop(0, steps, decode, jnp.zeros((BLOCK, cols), F32))
         recon = (total + bias_ref[...]).astype(BF16)
         recon_ref[at, :] = recon
         error = (recon.astype(F32) - acts_ref[at, :].astype(F32)).astype(BF16)
 
         def gradient(q, carry):
-            s = q * 4
+            s = q * EIGHT
             part = lax.dot_general(lhs_ref[q], error, (((0,), (0,)), ((), ())), preferred_element_type=F32)
-            for k in range(4):
+            for k in range(EIGHT):
                 to = pl.ds(place(active_ref[r, s + k]), BLOCK)
                 total_ref[to, :] += part[k * BLOCK : (k + 1) * BLOCK]
             return carry
 
-        lax.fori_loop(0, quads, gradient, 0)
+        lax.fori_loop(0, steps, gradient, 0)
         return carry
 
     lax.fori_loop(0, counts_ref.shape[0], row_block, 0)
@@ -146,26 +160,30 @@
     lax.fori_loop(0, rows // step, narrow, 0)
 
 
-def column_slice(active, slot, counts, packed, dec, acts, bias):
+def column_slice(active, slot, counts, pieces, dec, acts, bias):
     rows, cols = dec.shape
     tokens = acts.shape[0]
     slots = active.shape[1]
     smem = pl.BlockSpec(memory_space=pltpu.SMEM)
     vmem = pl.BlockSpec(memory_space=pltpu.VMEM)
+    anywhere = pl.BlockSpec(memory_space=pl.ANY)
     return pl.pallas_call(
         slice_kernel,
         out_shape=(
             jax.ShapeDtypeStruct((tokens, cols), BF16),
             jax.ShapeDtypeStruct((rows, cols), BF16),
         ),
-        in_specs=[smem, smem, smem, vmem, vmem, vmem, vmem],
+        in_specs=[smem, smem, smem, vmem, vmem] + [anywhere] * (1 + len(pieces)),
         out_specs=(vmem, vmem),
         scratch_shapes=[
-            pltpu.VMEM((slots // 4, BLOCK, 4 * BLOCK), BF16),
+            pltpu.VMEM((len(pieces) * pieces[0].shape[0], 2 * BLOCK), BF16),
+            pltpu.VMEM((rows, cols), BF16),
+            pltpu.VMEM((slots // EIGHT, BLOCK, EIGHT * BLOCK), BF16),
             pltpu.VMEM((rows, cols), F32),
+            pltpu.SemaphoreType.DMA((len(pieces) + 1,)),
         ],
-        compiler_params=pltpu.CompilerParams(vmem_limit_bytes=56 * 2**20),
-    )(active, slot, counts, packed, dec, acts, bias)
+        compiler_params=pltpu.CompilerParams(vmem_limit_bytes=52 * 2**20),
+    )(active, slot, counts, acts, bias, dec, *pieces)
 
 
 def body(acts, enc_weight, enc_bias, dec_weight, dec_bias, active, counts):
@@ -187,7 +205,6 @@
     mine = lax.dynamic_slice_in_dim(dec_weight, my_group * part, part, axis=0)
     mine = mine.reshape(part, n_index, cols).transpose(1, 0, 2)
     mine = lax.all_to_all(mine, "index", 0, 0, tiled=True)
-    dec_cols = lax.all_gather(mine.reshape(n_index * part, cols), "group", axis=0, tiled=True)
 
     slots = jnp.arange(active.shape[1])[None, :] < counts[:, None]
     is_block = active[:, :, None] == jnp.arange(n_blocks)[None, None, :]
@@ -220,14 +237,14 @@
     codes_any = jnp.maximum(preact, 0.0).astype(BF16)
 
     def packed_path():
+        dec_cols = lax.all_gather(mine.reshape(n_index * part, cols), "group", axis=0, tiled=True)
         packed = pack(pairs, codes_any)
         n = packed.shape[0] // 2
-        one = ring_gather(ring_gather(packed[:n], "x"), "z")
-        two = ring_gather(ring_gather(packed[n:], "z"), "x")
-        packed = jnp.concatenate([one, two], axis=0)
+        near = [jnp.concatenate(parts, axis=0) for parts in ring_gather([packed[:n], packed[n:]], ("x", "z"))]
+        one, two = ring_gather(near, ("z", "x"))
         acts_cols = lax.dynamic_slice_in_dim(rows, my_index * cols, cols, axis=1)
         bias_cols = lax.dynamic_slice_in_dim(dec_bias, my_index * cols, cols, axis=0)[None, :]
-        recon, grad = column_slice(active, slot, counts, packed, dec_cols, acts_cols, bias_cols)
+        recon, grad = column_slice(active, slot, counts, one + two, dec_cols, acts_cols, bias_cols)
         grad = lax.psum_scatter(grad, "group", scatter_dimension=0, tiled=True)
         recon = lax.all_to_all(recon.reshape(n_index, tok_dev, cols), "index", 0, 0, tiled=True)
         grad = lax.all_to_all(grad.reshape(n_index, part, cols), "index", 0, 0, tiled=True)

time: 359 us -> 298 us (0.83)
  blocking collectives: 54.2 us -> 21.6 us
  local copies, waits for them, and re-layouts: 22.8 us -> 8.61 us
  starting transfers between devices: 42.7 us -> 30 us
  Pallas kernels: 49.6 us -> 37.5 us
  waiting for transfers between devices: 157 us -> 166 us
    all_gather x1, waiting for transfers between devices: 37.5 us -> 0.01 us  [packed_path(): lax.all_gather(mine.reshape(n_index * part, cols), 'group', axis=0, tiled...]
    all_to_all x1 -> x0, blocking collectives: 27.5 us -> none  [body(): mine = lax.all_to_all(mine, 'index', 0, 0, tiled=True)]
    all_gather x1, waiting for transfers between devices: 35.7 us -> 62.2 us  [body(): rows = lax.all_gather(acts, 'index', axis=0, tiled=True)]
    ppermute x12, starting transfers between devices: 35.9 us -> 15.7 us  [hop(): return lax.ppermute(block, AXES, RINGS[axis])]
    ppermute x12, waiting for transfers between devices: 23.8 us -> 39.4 us  [hop(): return lax.ppermute(block, AXES, RINGS[axis])]
    pallas_call x1, Pallas kernels: 45.3 us -> 33.2 us  [column_slice(): pl.pallas_call(slice_kernel, out_shape=(jax.ShapeDtypeStruct((tokens, col...]
    another operation x16 -> x9, local copies, waits for them, and re-layouts: 11.8 us -> 1.33 us
    all_to_all x0 -> x1, starting transfers between devices: none -> 7.6 us  [body(): mine = lax.all_to_all(mine, 'index', 0, 0, tiled=True)]
  transfers between devices with their start and end apart: 16 -> 17, of which waited for: 11 -> 15; matrix products, arithmetic and copies ran while one was open for 9% -> 8% of each run, Pallas kernels for 0% -> 1%
where the time goes in v2:
time: 298 us; the launch traced here: 296 us
  waiting for transfers between devices  166 us (56%)
  Pallas kernels  37.5 us (13%)
  starting transfers between devices  30 us (10%)
  blocking collectives  21.6 us (7%)
  between operations  14.5 us (5%)
  matrix products  13.8 us (5%)
  local copies, waits for them, and re-layouts  8.61 us (3%)
  other arithmetic  3.93 us (1%)
    all_gather x1, waiting for transfers between devices, body(): rows = lax.all_gather(acts, 'index', axis=0, tiled=True)  62.2 us
    reduce_scatter x1, waiting for transfers between devices, packed_path(): grad = lax.psum_scatter(grad, 'group', scatter_dimension=0, tiled=True)  44.4 us
    ppermute x12, waiting for transfers between devices, hop(): return lax.ppermute(block, AXES, RINGS[axis])  39.4 us
    pallas_call x1, Pallas kernels, column_slice(): pl.pallas_call(slice_kernel, out_shape=(jax.ShapeDtypeStruct((tokens, col...  33.2 us
    all_to_all x1, waiting for transfers between devices, packed_path(): lax.all_to_all(grad.reshape(n_index, part, cols), 'index', 0, 0, tiled=True)  19.2 us
    ppermute x12, starting transfers between devices, hop(): return lax.ppermute(block, AXES, RINGS[axis])  15.7 us
    all_to_all x1, blocking collectives, packed_path(): lax.all_to_all(recon.reshape(n_index, tok_dev, cols), 'index', 0, 0, tile...  13.8 us
    dot_general x1, matrix products, body(): preact = jnp.dot(rows, enc_weight, preferred_element_type=F32) + enc_bias  13.7 us
  transfers between devices with their start and end apart: 17, of which 15 were waited for; matrix products, arithmetic and copies ran while one was open for 8% of the time, Pallas kernels for 1%

profile of v2, /device:TPU:9, one launch (start us, length us, event | category | flops | bytes accessed | tf_op | source)
XLA Modules:
  0.0 296.3 jit_solution(18432990910173447824)
XLA Ops:
  9.9 1.3 constant_dynamic-slice_fusion.3
  11.2 1.3 copy.19
  13.4 7.6 %all-to-all-start.2 = ((bf16[16,128,256]{1,2,0:T(8,128)(2,1)}), bf16[16,128,256]{1,2,0:T(8,128)(2,1)S(1)}, u32[]{:S(2)}, u32[]{:S(2)}) async-start(bf16[16,128,256]{1,2,0:T(8,128)(2,1)} %bitcast.11), calls=%async_computation.5 | async-start | bytes 2097152 | tf_op jit(solution)/shard_map/all_to_all | solution.py:207
  21.0 7.8 %pmax.7 = s32[]{:T(128)} all-reduce(s32[]{:T(128)} %slice_reduce_fusion), channel_id=1, replica_groups=mesh['group'=8,'index'=16] {'group'}, use_global_device_ids=true, to_apply=%region_2.3 | all-reduce | flops 1 | bytes 8 | tf_op jit(solution)/shard_map/pmax | solution.py:217
  29.7 62.2 %all-gather.8.cloned.1.call-done = bf16[1024,4096]{1,0:T(8,128)(2,1)} async-done(((bf16[64,4096]{1,0:T(8,128)(2,1)}), bf16[1024,4096]{1,0:T(8,128)(2,1)}) %all-gather.8.cloned.1.call-update) | async-done | bytes 8388624 | tf_op jit(solution)/shard_map/all_gather | solution.py:203
  91.9 13.7 %maximum_convert_fusion = bf16[1024,1024]{1,0:T(8,128)(2,1)S(1)} fusion(f32[1024]{0:T(1024)S(1)} %copy-done.9, bf16[1024,4096]{1,0:T(8,128)(2,1)} %all-gather.8.cloned.1.call-done, bf16[4096,1024]{1,0:T(8,128)(2,1)} %param.10), kind=kOutput, calls=%fused_computation.14 | convolution fusion | flops 8593080320 | bytes 18878464 | tf_op jit(solution)/shard_map/dot_general | solution.py:236
  105.6 184.2 %conditional.3 = (bf16[64,4096]{1,0:T(8,128)(2,1)}, f32[128,4096]{1,0:T(8,128)}) conditional(s32[]{:T(128)} %convert_element_type.41, (s32[]{:T(128)}, pred[16,256]{1,0:T(8,128)(4,1)S(1)}, bf16[1024,1024]{1,0:T(8,128)(2,1)S(1)}, bf16[1024,4096]{1,0:T(8,128)(2,1)}, f32[4096]{0:T(1024)S(1)}, /*index=5*/bf16[64,4096]{1,0:T(8,128)(2,1)}) %tuple.67, ...), branch_computations={%region_3.6_spmd, %region_6.10_spmd} | conditional | flops 17191665664 | bytes 147932192
  105.9 1.3 copy.18
  107.4 4.3 %branch_1_fun.2 = bf16[1536,128]{1,0:T(8,128)(2,1)S(1)} custom-call(s32[48]{0:T(128)S(1)} %select_reduce_fusion.1.pair_ref, bf16[1024,1024]{1,0:T(8,128)(2,1)S(1)} %get-tuple-element.90.codes_ref), custom_call_target="tpu_custom_call" | custom-call | tf_op jit(solution)/shard_map/cond/branch_1_fun/pallas_call | solution.py:73
  111.7 2.5 collective-permute-start.1
  114.8 2.0 collective-permute-done.1
  116.8 2.2 collective-permute-done
  119.0 1.8 collective-permute-start.2
  121.4 2.5 collective-permute-done.2
  123.9 1.8 collective-permute-done.3
  127.4 3.2 %collective-permute-done.4 = bf16[768,128]{1,0:T(8,128)(2,1)S(1)} collective-permute-done((bf16[768,128]{1,0:T(8,128)(2,1)S(1)}, bf16[768,128]{1,0:T(8,128)(2,1)S(1)}, u32[]{:S(2)}, u32[]{:S(2)}) %collective-permute-start.4) | collective-permute-done | bytes 196640 | tf_op jit(solution)/shard_map/cond/branch_1_fun/ppermute | solution.py:41
  132.5 1.2 collective-permute-start.6
  133.6 9.3 %collective-permute-done.7.refs_7_ = bf16[3072,128]{1,0:T(8,128)(2,1)S(1)} collective-permute-done((bf16[3072,128]{1,0:T(8,128)(2,1)S(1)}, bf16[3072,128]{1,0:T(8,128)(2,1)S(1)}, u32[]{:S(2)}, u32[]{:S(2)}) %collective-permute-start.7) | collective-permute-done | bytes 786464 | tf_op jit(solution)/shard_map/cond/branch_1_fun/ppermute | solution.py:41
  143.7 2.3 collective-permute-start.8
  146.0 1.5 collective-permute-start.9
  147.5 7.5 %collective-permute-done.8.refs_2_ = bf16[3072,128]{1,0:T(8,128)(2,1)} collective-permute-done((bf16[3072,128]{1,0:T(8,128)(2,1)S(1)}, bf16[3072,128]{1,0:T(8,128)(2,1)}, u32[]{:S(2)}, u32[]{:S(2)}) %collective-permute-start.8) | collective-permute-done | bytes 786464 | tf_op jit(solution)/shard_map/cond/branch_1_fun/ppermute | solution.py:41
  154.9 2.3 collective-permute-done.9.refs_6_
  157.2 1.2 collective-permute-start.10
  158.4 1.5 collective-permute-start.11
  162.9 5.8 %collective-permute-done.10.refs_1_ = bf16[3072,128]{1,0:T(8,128)(2,1)} collective-permute-done((bf16[3072,128]{1,0:T(8,128)(2,1)}, bf16[3072,128]{1,0:T(8,128)(2,1)}, u32[]{:S(2)}, u32[]{:S(2)}) %collective-permute-start.10) | collective-permute-done | bytes 786464 | tf_op jit(solution)/shard_map/cond/branch_1_fun/ppermute | solution.py:41
  168.7 1.2 collective-permute-done.11.refs_5_
  169.9 33.2 %branch_1_fun.3 = (bf16[1024,256]{1,0:T(8,128)(2,1)S(1)}, bf16[16384,256]{1,0:T(8,128)(2,1)}) custom-call(s32[16,32]{1,0:T(8,128)S(1)} %get-tuple-element.78.active_ref, s32[16,32]{1,0:T(8,128)S(1)} %broadcast_clamp_fusion.slot_ref, s32[16]{0:T(128)S(1)} %copy-done.8, bf16[1024,256]{1,0:T(8,128)(2,1)S(1)} %constant_dynamic-slice_fusion.1.acts_ref, ...), custom_call_target="tpu_custom_call" | custom-call | tf_op jit(solution)/shard_map/cond/branch_1_fun/pallas_call | solution.py:170
  203.1 13.8 %all_to_all.13 = bf16[16,64,256]{2,1,0:T(8,128)(2,1)S(1)} all-to-all(bf16[16,64,256]{2,1,0:T(8,128)(2,1)S(1)} %bitcast.30), channel_id=1, replica_groups=mesh['group'=8,'index'=16] {'index'}, dimensions={0} | all-to-all | bytes 1048576 | tf_op jit(solution)/shard_map/cond/branch_1_fun/all_to_all | solution.py:249
  216.9 44.4 %reduce-scatter.8.cloned.1.call-done = bf16[2048,256]{1,0:T(8,128)(2,1)} async-done(((bf16[16384,256]{1,0:T(8,128)(2,1)}), bf16[2048,256]{1,0:T(8,128)(2,1)}) %reduce-scatter.8.cloned.1.call-update) | async-done | bytes 1048592 | tf_op jit(solution)/shard_map/cond/branch_1_fun/reduce_scatter | solution.py:248
  261.3 6.7 %all-to-all-start.1 = ((bf16[16,128,256]{2,1,0:T(8,128)(2,1)}), bf16[16,128,256]{2,1,0:T(8,128)(2,1)S(1)}, u32[]{:S(2)}, u32[]{:S(2)}) async-start(bf16[16,128,256]{2,1,0:T(8,128)(2,1)} %bitcast.35), calls=%async_computation.2 | async-start | bytes 2097152 | tf_op jit(solution)/shard_map/cond/branch_1_fun/all_to_all | solution.py:250
  268.8 19.2 %all-to-all-done.1 = bf16[16,128,256]{2,1,0:T(8,128)(2,1)S(1)} async-done(((bf16[16,128,256]{2,1,0:T(8,128)(2,1)}), bf16[16,128,256]{2,1,0:T(8,128)(2,1)S(1)}, u32[]{:S(2)}, u32[]{:S(2)}) %all-to-all-start.1) | async-done | bytes 1048608 | tf_op jit(solution)/shard_map/cond/branch_1_fun/all_to_all | solution.py:250
  288.2 1.5 copy.21
  (53 shorter events, 13.5 us)
Async XLA Ops:
  7.2 84.7 %copy-start.9 = (f32[1024]{0:T(1024)S(1)}, f32[1024]{0:T(1024)}, u32[]{:S(2)}) copy-start(f32[1024]{0:T(1024)} %param.11) | copy-start | bytes 12292
  7.2 84.7 %all-gather.8.cloned.1.call-start = ((), (), s32[]{:S(2)}) async-start(), calls=%async_computation.11 | async-start | bytes 8912896 | tf_op jit(solution)/shard_map/all_gather | solution.py:203
  13.4 92.1 %all-to-all-start.2 = ((bf16[16,128,256]{1,2,0:T(8,128)(2,1)}), bf16[16,128,256]{1,2,0:T(8,128)(2,1)S(1)}, u32[]{:S(2)}, u32[]{:S(2)}) async-start(bf16[16,128,256]{1,2,0:T(8,128)(2,1)} %bitcast.11), calls=%async_computation.5 | async-start | bytes 2097152 | tf_op jit(solution)/shard_map/all_to_all | solution.py:207
  29.6 75.9 %copy-start.6 = (s32[16,32]{1,0:T(8,128)S(1)}, s32[16,32]{1,0:T(8,128)}, u32[]{:S(2)}) copy-start(s32[16,32]{1,0:T(8,128)} %param.14) | copy-start | bytes 6148
  29.6 75.9 %copy-start.7 = (f32[4096]{0:T(1024)S(1)}, f32[4096]{0:T(1024)}, u32[]{:S(2)}) copy-start(f32[4096]{0:T(1024)} %param.13) | copy-start | bytes 49156
  105.8 64.1 %all-gather.6.cloned.1.call-start = ((), (), s32[]{:S(2)}) async-start(), calls=%async_computation.9 | async-start | bytes 9437184 | tf_op jit(solution)/shard_map/cond/branch_1_fun/all_gather | solution.py:240
  107.2 62.7 %copy-start.8 = (s32[16]{0:T(128)S(1)}, s32[16]{0:T(128)}, u32[]{:S(2)}) copy-start(s32[16]{0:T(128)} %get-tuple-element.81.counts_ref) | copy-start | bytes 196 | tf_op jit(solution)/shard_map/conditional.1
  107.2 154.1 %reduce-scatter.8.cloned.1.call-start = ((), (), s32[]{:S(2)}) async-start(), calls=%async_computation.10 | async-start | bytes 9437184 | tf_op jit(solution)/shard_map/cond/branch_1_fun/reduce_scatter | solution.py:248
  111.7 5.1 %collective-permute-start.1 = (bf16[768,128]{1,0:T(8,128)(2,1)S(1)}, bf16[768,128]{1,0:T(8,128)(2,1)S(1)}, u32[]{:S(2)}, u32[]{:S(2)}) collective-permute-start(bf16[768,128]{1,0:T(8,128)(2,1)S(1)} %get-tuple-element.129), channel_id=1, source_target_pairs={{0,4},{1,5},{2,6},{3,7},{4,8},{5,9},{6,10},{7,11},{8,12},{9,13},{1... | collective-permute-start | bytes 589832 | tf_op jit(solution)/shard_map/cond/branch_1_fun/ppermute | solution.py:41
  114.2 4.8 %collective-permute-start = (bf16[768,128]{1,0:T(8,128)(2,1)S(1)}, bf16[768,128]{1,0:T(8,128)(2,1)S(1)}, u32[]{:S(2)}, u32[]{:S(2)}) collective-permute-start(bf16[768,128]{1,0:T(8,128)(2,1)S(1)} %get-tuple-element.130), channel_id=1, source_target_pairs={{0,1},{1,2},{2,3},{3,0},{4,5},{5,6},{6,7},{7,4},{8,9},{9,10},{10,1... | collective-permute-start | bytes 589832 | tf_op jit(solution)/shard_map/cond/branch_1_fun/ppermute | solution.py:41
  119.0 4.9 %collective-permute-start.2 = (bf16[768,128]{1,0:T(8,128)(2,1)S(1)}, bf16[768,128]{1,0:T(8,128)(2,1)S(1)}, u32[]{:S(2)}, u32[]{:S(2)}) collective-permute-start(bf16[768,128]{1,0:T(8,128)(2,1)S(1)} %collective-permute-done), channel_id=1, source_target_pairs={{0,1},{1,2},{2,3},{3,0},{4,5},{5,6},{6,7},{7,4},{8,9},{9,10},{10,1... | collective-permute-start | bytes 589832 | tf_op jit(solution)/shard_map/cond/branch_1_fun/ppermute | solution.py:41
  120.8 4.9 %collective-permute-start.3 = (bf16[768,128]{1,0:T(8,128)(2,1)S(1)}, bf16[768,128]{1,0:T(8,128)(2,1)S(1)}, u32[]{:S(2)}, u32[]{:S(2)}) collective-permute-start(bf16[768,128]{1,0:T(8,128)(2,1)S(1)} %collective-permute-done.1), channel_id=1, source_target_pairs={{0,4},{1,5},{2,6},{3,7},{4,8},{5,9},{6,10},{7,11},{8,12},{9,13},{1... | collective-permute-start | bytes 589832 | tf_op jit(solution)/shard_map/cond/branch_1_fun/ppermute | solution.py:41
  125.7 4.9 %collective-permute-start.4 = (bf16[768,128]{1,0:T(8,128)(2,1)S(1)}, bf16[768,128]{1,0:T(8,128)(2,1)S(1)}, u32[]{:S(2)}, u32[]{:S(2)}) collective-permute-start(bf16[768,128]{1,0:T(8,128)(2,1)S(1)} %collective-permute-done.2), channel_id=1, source_target_pairs={{0,1},{1,2},{2,3},{3,0},{4,5},{5,6},{6,7},{7,4},{8,9},{9,10},{10,1... | collective-permute-start | bytes 589832 | tf_op jit(solution)/shard_map/cond/branch_1_fun/ppermute | solution.py:41
  126.5 4.9 %collective-permute-start.5 = (bf16[768,128]{1,0:T(8,128)(2,1)S(1)}, bf16[768,128]{1,0:T(8,128)(2,1)S(1)}, u32[]{:S(2)}, u32[]{:S(2)}) collective-permute-start(bf16[768,128]{1,0:T(8,128)(2,1)S(1)} %collective-permute-done.3), channel_id=1, source_target_pairs={{0,4},{1,5},{2,6},{3,7},{4,8},{5,9},{6,10},{7,11},{8,12},{9,13},{1... | collective-permute-start | bytes 589832 | tf_op jit(solution)/shard_map/cond/branch_1_fun/ppermute | solution.py:41
  131.6 38.3 %copy-start = (bf16[3072,128]{1,0:T(8,128)(2,1)}, bf16[3072,128]{1,0:T(8,128)(2,1)S(1)}, u32[]{:S(2)}) copy-start(bf16[3072,128]{1,0:T(8,128)(2,1)S(1)} %pad_maximum_fusion.1.refs_4_) | copy-start | bytes 2359300 | tf_op jit(solution)/shard_map/conditional.1
  131.6 11.3 %collective-permute-start.7 = (bf16[3072,128]{1,0:T(8,128)(2,1)S(1)}, bf16[3072,128]{1,0:T(8,128)(2,1)S(1)}, u32[]{:S(2)}, u32[]{:S(2)}) collective-permute-start(bf16[3072,128]{1,0:T(8,128)(2,1)S(1)} %pad_maximum_fusion.1.refs_4_), channel_id=1, source_target_pairs={{0,1},{1,2},{2,3},{3,0},{4,5},{5,6},{6,7},{7,4},{8,9},{9,10},{10,1... | collective-permute-start | bytes 2359304 | tf_op jit(solution)/shard_map/cond/branch_1_fun/ppermute | solution.py:41
  132.5 11.2 %collective-permute-start.6 = (bf16[3072,128]{1,0:T(8,128)(2,1)S(1)}, bf16[3072,128]{1,0:T(8,128)(2,1)S(1)}, u32[]{:S(2)}, u32[]{:S(2)}) collective-permute-start(bf16[3072,128]{1,0:T(8,128)(2,1)S(1)} %pad_maximum_fusion.refs_0_), channel_id=1, source_target_pairs={{0,4},{1,5},{2,6},{3,7},{4,8},{5,9},{6,10},{7,11},{8,12},{9,13},{1... | collective-permute-start | bytes 2359304 | tf_op jit(solution)/shard_map/cond/branch_1_fun/ppermute | solution.py:41
  142.9 27.0 %copy-start.4 = (bf16[3072,128]{1,0:T(8,128)(2,1)}, bf16[3072,128]{1,0:T(8,128)(2,1)S(1)}, u32[]{:S(2)}) copy-start(bf16[3072,128]{1,0:T(8,128)(2,1)S(1)} %collective-permute-done.7.refs_7_) | copy-start | bytes 2359300 | tf_op jit(solution)/shard_map/conditional.1
  143.7 16.9 %copy-start.5 = (bf16[3072,128]{1,0:T(8,128)(2,1)}, bf16[3072,128]{1,0:T(8,128)(2,1)S(1)}, u32[]{:S(2)}) copy-start(bf16[3072,128]{1,0:T(8,128)(2,1)S(1)} %collective-permute-done.6.refs_3_) | copy-start | bytes 2359300 | tf_op jit(solution)/shard_map/conditional.1
  143.7 11.2 %collective-permute-start.8 = (bf16[3072,128]{1,0:T(8,128)(2,1)S(1)}, bf16[3072,128]{1,0:T(8,128)(2,1)}, u32[]{:S(2)}, u32[]{:S(2)}) collective-permute-start(bf16[3072,128]{1,0:T(8,128)(2,1)S(1)} %collective-permute-done.6.refs_3_), channel_id=1, source_target_pairs={{0,4},{1,5},{2,6},{3,7},{4,8},{5,9},{6,10},{7,11},{8,12},{9,13},{1... | collective-permute-start | bytes 2359304 | tf_op jit(solution)/shard_map/cond/branch_1_fun/ppermute | solution.py:41
  146.0 11.2 %collective-permute-start.9 = (bf16[3072,128]{1,0:T(8,128)(2,1)S(1)}, bf16[3072,128]{1,0:T(8,128)(2,1)}, u32[]{:S(2)}, u32[]{:S(2)}) collective-permute-start(bf16[3072,128]{1,0:T(8,128)(2,1)S(1)} %collective-permute-done.7.refs_7_), channel_id=1, source_target_pairs={{0,1},{1,2},{2,3},{3,0},{4,5},{5,6},{6,7},{7,4},{8,9},{9,10},{10,1... | collective-permute-start | bytes 2359304 | tf_op jit(solution)/shard_map/cond/branch_1_fun/ppermute | solution.py:41
  157.2 11.5 %collective-permute-start.10 = (bf16[3072,128]{1,0:T(8,128)(2,1)}, bf16[3072,128]{1,0:T(8,128)(2,1)}, u32[]{:S(2)}, u32[]{:S(2)}) collective-permute-start(bf16[3072,128]{1,0:T(8,128)(2,1)} %collective-permute-done.8.refs_2_), channel_id=1, source_target_pairs={{0,4},{1,5},{2,6},{3,7},{4,8},{5,9},{6,10},{7,11},{8,12},{9,13},{1... | collective-permute-start | bytes 2359304 | tf_op jit(solution)/shard_map/cond/branch_1_fun/ppermute | solution.py:41
  158.4 11.5 %collective-permute-start.11 = (bf16[3072,128]{1,0:T(8,128)(2,1)}, bf16[3072,128]{1,0:T(8,128)(2,1)}, u32[]{:S(2)}, u32[]{:S(2)}) collective-permute-start(bf16[3072,128]{1,0:T(8,128)(2,1)} %collective-permute-done.9.refs_6_), channel_id=1, source_target_pairs={{0,1},{1,2},{2,3},{3,0},{4,5},{5,6},{6,7},{7,4},{8,9},{9,10},{10,1... | collective-permute-start | bytes 2359304 | tf_op jit(solution)/shard_map/cond/branch_1_fun/ppermute | solution.py:41
  261.3 26.7 %all-to-all-start.1 = ((bf16[16,128,256]{2,1,0:T(8,128)(2,1)}), bf16[16,128,256]{2,1,0:T(8,128)(2,1)S(1)}, u32[]{:S(2)}, u32[]{:S(2)}) async-start(bf16[16,128,256]{2,1,0:T(8,128)(2,1)} %bitcast.35), calls=%async_computation.2 | async-start | bytes 2097152 | tf_op jit(solution)/shard_map/cond/branch_1_fun/all_to_all | solution.py:250
Sparse Core Ops, SparseCore 0:
  10.1 81.6 all-gather.7
  109.0 48.9 all-gather.5
  203.3 58.0 reduce-scatter.7
